TPU v7x, 128 devices: a whole 4x4x4 slice. The times are simulated.
128 devices in a mesh: dp: 16 (over y, x_lo, core), narrow: 8 (over z, x_hi).
Axes of the slice: x: 4 (x_hi: 2, x_lo: 2; x = x_hi * 2 + x_lo), y: 4, z: 4, core: 2. Of those that a mesh axis runs over, the one named last changes fastest.
Arguments:
- embeddings: bfloat16 [262144, 128], P(('dp', 'narrow')), may hold values from -6 to 6
- cluster_id: int32 [262144], P(('dp', 'narrow')), may hold values from 0 to 31, as said below
- member_rank: int32 [262144], P(('dp', 'narrow')), may hold values from 0 to 12287, as said below
- cluster_size: int32 [32], replicated, may hold values from 4096 to 12288, as said below
- cluster_owner: int32 [32], replicated, may hold values from 0 to 15, as said below
Outputs:
- similar: float32 [262144], P(('dp', 'narrow'))
Inputs may be any that keep to these rules, and one draw needn't show every extreme that they name: `member_rank`: ranks of one cluster are 0 to its size - 1, each held by exactly one row; a cluster of owner g occupies the slots g * 2048 * 8 + offset + rank, where offset is the total size of the clusters of the same owner with smaller ids; slot s lies with device s // 2048 of the mesh order. `cluster_id`: of the rows of one device, at most 32 have slots on any one device, and exactly 32 for some pair of devices. `cluster_size`: the sizes of the clusters of one owner sum to 2048 * 8. `cluster_owner`: every group owns exactly 2 clusters.
All inputs are finite; a program needn't handle non-finite values.
Results may differ from a plain program's by a relative error of at most 0.0013.
Values may be sent and summed in bfloat16 or wider, within the bound.
A program may use at most 64 MiB of HBM per device.

v0:
```python
import jax
import jax.numpy as jnp
from jax import lax
from jax.sharding import PartitionSpec as P


def cluster_tables(cluster_size, cluster_owner):
    cluster_count = cluster_size.shape[0]
    cluster_ids = jnp.arange(cluster_count, dtype=jnp.int32)
    same_owner = cluster_owner[None, :] == cluster_owner[:, None]
    earlier_ids = same_owner & (cluster_ids[None, :] < cluster_ids[:, None])
    offset = jnp.sum(jnp.where(earlier_ids, cluster_size[None, :], 0), axis=1)
    return (cluster_ids, offset)


def slot_cluster(slot_index, group_index, cluster_ids, offset, cluster_size, cluster_owner):
    inside = (
        (cluster_owner[None, :] == group_index)
        & (slot_index[:, None] >= offset[None, :])
        & (slot_index[:, None] < offset[None, :] + cluster_size[None, :])
    )
    cluster_pick = jnp.sum(jnp.where(inside, cluster_ids[None, :], 0), axis=1)
    return jnp.where(jnp.any(inside, axis=1), cluster_pick, -1)


def fold_block(
    best_score, local_rows, row_slot, row_cluster, column_piece, group_index, tables, block_rows
):
    col_slot = jnp.arange(column_piece.shape[0], dtype=jnp.int32)
    col_cluster = slot_cluster(col_slot, group_index, *tables)
    block_count = local_rows.shape[0] // block_rows

    def per_block(operands):
        row_block, slot_block, label_block, best_block = operands
        scores = jnp.einsum(
            "rk,ck->rc", row_block, column_piece, preferred_element_type=jnp.float32
        )
        allowed = (col_slot[None, :] < slot_block[:, None]) & (
            col_cluster[None, :] == label_block[:, None]
        )
        block_top = jnp.max(jnp.where(allowed, scores, -1.0), axis=1)
        return jnp.maximum(best_block, block_top)

    merged = lax.map(
        per_block,
        (
            local_rows.reshape(block_count, block_rows, -1),
            row_slot.reshape(block_count, block_rows),
            row_cluster.reshape(block_count, block_rows),
            best_score.reshape(block_count, block_rows),
        ),
    )
    return merged.reshape(-1)


def shards(embeddings, cluster_id, member_rank, cluster_size, cluster_owner):
    rows_dev = embeddings.shape[0]
    features = embeddings.shape[1]
    groups = lax.axis_size("dp")
    narrow_size = lax.axis_size("narrow")
    devices = groups * narrow_size
    capacity = 2 * rows_dev // devices
    group_rows = rows_dev * narrow_size
    widened = embeddings.astype(jnp.float32)
    normed = (
        widened * lax.rsqrt(jnp.sum(widened * widened, axis=1, keepdims=True) + 1e-06)
    ).astype(jnp.bfloat16)
    cluster_ids, offset = cluster_tables(cluster_size, cluster_owner)
    member = cluster_id[:, None] == cluster_ids[None, :]
    owner_row = jnp.sum(jnp.where(member, cluster_owner[None, :], 0), axis=1)
    offset_row = jnp.sum(jnp.where(member, offset[None, :], 0), axis=1)
    target = owner_row * group_rows + offset_row + member_rank
    destination = target // rows_dev
    local_slot = target % rows_dev
    chosen = (destination[:, None] == jnp.arange(devices, dtype=jnp.int32)[None, :]).astype(
        jnp.int32
    )
    position = jnp.sum((jnp.cumsum(chosen, axis=0) - 1) * chosen, axis=1)
    flat_index = destination * capacity + position
    outgoing = jnp.zeros((devices * capacity, features), jnp.bfloat16).at[flat_index].set(normed)
    out_slot = jnp.full((devices * capacity,), rows_dev, jnp.int32).at[flat_index].set(local_slot)
    arrived, in_slot = (
        lax.all_to_all(
            outgoing.reshape(devices, capacity, features),
            ("dp", "narrow"),
            split_axis=0,
            concat_axis=0,
            tiled=True,
        ),
        lax.all_to_all(
            out_slot.reshape(devices, capacity),
            ("dp", "narrow"),
            split_axis=0,
            concat_axis=0,
            tiled=True,
        ),
    )
    arrived = arrived.reshape(devices * capacity, features)
    in_slot = in_slot.reshape(-1)
    local_rows = jnp.zeros((rows_dev, features), jnp.bfloat16).at[in_slot].set(arrived, mode="drop")
    group_index = lax.axis_index("dp")
    narrow_index = lax.axis_index("narrow")
    row_slot = narrow_index * rows_dev + jnp.arange(rows_dev, dtype=jnp.int32)
    tables = (cluster_ids, offset, cluster_size, cluster_owner)
    row_cluster = slot_cluster(row_slot, group_index, *tables)
    block_rows = min(512, rows_dev)
    best_score = jnp.full((rows_dev,), -1.0, jnp.float32)
    best_score = fold_block(
        best_score,
        local_rows,
        row_slot,
        row_cluster,
        lax.all_gather(local_rows, "narrow", axis=0, tiled=True),
        group_index,
        tables,
        block_rows,
    )
    answer = best_score[jnp.minimum(in_slot, rows_dev - 1)]
    returned = lax.all_to_all(
        answer.reshape(devices, capacity), ("dp", "narrow"), split_axis=0, concat_axis=0, tiled=True
    )
    return returned.reshape(-1)[flat_index]


def solution(mesh):
    in_specs = (P(("dp", "narrow"), None), P(("dp", "narrow")), P(("dp", "narrow")), P(), P())
    out_specs = P(("dp", "narrow"))
    return jax.shard_map(shards, mesh=mesh, in_specs=in_specs, out_specs=out_specs, check_vma=False)
```

profile of v0, /device:TPU:1, one launch (start us, length us, event | category | flops | bytes accessed | tf_op | source)
XLA Modules:
  0.0 258.3 jit_solution(356469414178802188)
XLA Ops:
  6.5 0.0 copy-start
  6.5 0.9 select_reduce_fusion.5
  7.5 0.7 add.81
  8.1 0.7 broadcast_compare_fusion
  8.8 1.0 select_reduce_fusion.3
  9.8 0.7 add_select_fusion
  10.5 0.1 copy.12
  10.6 0.3 fusion.12
  11.0 0.1 add_add_fusion
  11.1 0.3 copy.13
  11.4 0.6 fusion.11
  12.0 8.1 %scatter_custom_fusion = s32[4096]{0:T(1024)S(1)} fusion(s32[2048]{0:T(1024)S(1)} %get-tuple-element.82, s32[2048]{0:T(1024)S(1)} %get-tuple-element.85, s32[]{:T(128)} %constant.72.clone.1), kind=kCustom, calls=%fused_computation.61 | custom fusion | bytes 16388 | tf_op jit(solution)/shard_map/scatter | solution.py:81
  20.1 0.7 all_to_all.15
  20.8 11.5 %all-to-all-start = ((s32[128,1,32]{2,1,0:T(1,128)}), s32[128,1,32]{2,1,0:T(1,128)S(1)}, u32[]{:S(2)}, u32[]{:S(2)}) async-start(s32[128,1,32]{2,1,0:T(1,128)} %bitcast.4), calls=%async_computation | async-start | bytes 131072 | tf_op jit(solution)/shard_map/all_to_all | solution.py:90
  32.3 0.0 copy-done
  32.3 0.3 fusion.9
  32.7 7.8 %scatter_custom_fusion.1 = bf16[4096,128]{1,0:T(8,128)(2,1)} fusion(s32[2048]{0:T(1024)S(1)} %get-tuple-element.82, bf16[2048,128]{1,0:T(8,128)(2,1)S(1)} %copy-done, f32[2048]{0:T(1024)S(1)} %add_rsqrt_fusion, bf16[]{:T(256)} %constant.71.clone.1), kind=kCustom, calls=%fused_computation.32 | custom fusion | flops 786432 | bytes 1581058 | tf_op jit(solution)/shard_map/scatter | solution.py:80
  40.5 1.7 all-to-all-done
  42.2 8.0 %all-to-all-start.1 = ((bf16[128,32,128]{2,1,0:T(8,128)(2,1)}), bf16[128,32,128]{2,1,0:T(8,128)(2,1)S(1)}, u32[]{:S(2)}, u32[]{:S(2)}) async-start(bf16[128,32,128]{2,1,0:T(8,128)(2,1)} %bitcast.6), calls=%async_computation.1 | async-start | bytes 2097152 | tf_op jit(solution)/shard_map/all_to_all | solution.py:83
  50.3 0.0 all-gather.2.cloned.1.call-start
  50.3 0.5 broadcast.157
  50.8 0.8 reduce.6
  51.6 0.1 reshape.137
  51.8 18.0 %all-to-all-done.1 = bf16[128,32,128]{2,1,0:T(8,128)(2,1)S(1)} async-done(((bf16[128,32,128]{2,1,0:T(8,128)(2,1)}), bf16[128,32,128]{2,1,0:T(8,128)(2,1)S(1)}, u32[]{:S(2)}, u32[]{:S(2)}) %all-to-all-start.1) | async-done | bytes 1048608 | tf_op jit(solution)/shard_map/all_to_all | solution.py:83
  69.8 11.6 %scatter_custom_fusion.2 = bf16[2048,128]{1,0:T(8,128)(2,1)} fusion(s32[4096]{0:T(1024)S(1)} %bitcast.44, bf16[4096,128]{1,0:T(8,128)(2,1)S(1)} %bitcast.37, bf16[]{:T(256)} %constant.71.clone.1), kind=kCustom, calls=%fused_computation.39 | custom fusion | bytes 524290 | tf_op jit(solution)/shard_map/scatter | solution.py:100
  81.3 0.0 all-gather.2.cloned.1.call-update
  81.4 0.2 fusion.21
  81.6 0.8 fusion.8
  82.4 1.0 select_reduce_fusion.1
  83.5 64.9 %all-gather.2.cloned.1.call-done = bf16[16384,128]{1,0:T(8,128)(2,1)} async-done(((bf16[2048,128]{1,0:T(8,128)(2,1)}), bf16[16384,128]{1,0:T(8,128)(2,1)}) %all-gather.2.cloned.1.call-update) | async-done | bytes 4194320 | tf_op jit(solution)/shard_map/all_gather | solution.py:113
  148.4 41.8 %while.11 = (s32[]{:T(128)}, f32[4,512]{1,0:T(4,128)S(1)}, s32[4,512]{1,0:T(4,128)S(1)}, s32[16384]{0:T(1024)S(1)}, s32[4,512]{1,0:T(4,128)S(1)}, /*index=5*/bf1...) while((s32[]{:T(128)}, f32[4,512]{1,0:T(4,128)S(1)}, ...), condition=%wide.region_16.17_spmd.clone, body=%wide.region_14.16_spmd.clone.sunk | while | flops 2189426688 | bytes 4414053 | solution.py:44
  148.4 10.3 %select_reduce_fusion.7 = f32[512]{0:T(512)S(1)} fusion(bf16[16384,128]{1,0:T(8,128)(2,1)} %get-tuple-element.160, s32[16384]{0:T(1024)S(1)} %get-tuple-element.157, s32[512]{0:T(512)S(1)} %bitcast.43, s32[512]{0:T(512)S(1)} %bitcast.42, bf16[4,512,128]{2,1,0:T(8,128)(2,1)} %get-tuple-element.159, s32[]{:T(128)} %get-tuple-element.145), kind=kOutput, calls=%fused_computation.7.clone.1 | convolution fusion | flops 2189426176 | bytes 4397568 | tf_op jit(solution)/shard_map/while/body/eval_jaxpr/rk,ck->rc/dot_general | solution.py:35
  158.8 0.1 dynamic_update_slice.6
  158.8 10.4 %select_reduce_fusion.7 = f32[512]{0:T(512)S(1)} fusion(bf16[16384,128]{1,0:T(8,128)(2,1)} %get-tuple-element.160, s32[16384]{0:T(1024)S(1)} %get-tuple-element.157, s32[512]{0:T(512)S(1)} %bitcast.43, s32[512]{0:T(512)S(1)} %bitcast.42, bf16[4,512,128]{2,1,0:T(8,128)(2,1)} %get-tuple-element.159, s32[]{:T(128)} %get-tuple-element.145), kind=kOutput, calls=%fused_computation.7.clone.1 | convolution fusion | flops 2189426176 | bytes 4397568 | tf_op jit(solution)/shard_map/while/body/eval_jaxpr/rk,ck->rc/dot_general | solution.py:35
  169.2 0.1 dynamic_update_slice.6
  169.3 10.4 %select_reduce_fusion.7 = f32[512]{0:T(512)S(1)} fusion(bf16[16384,128]{1,0:T(8,128)(2,1)} %get-tuple-element.160, s32[16384]{0:T(1024)S(1)} %get-tuple-element.157, s32[512]{0:T(512)S(1)} %bitcast.43, s32[512]{0:T(512)S(1)} %bitcast.42, bf16[4,512,128]{2,1,0:T(8,128)(2,1)} %get-tuple-element.159, s32[]{:T(128)} %get-tuple-element.145), kind=kOutput, calls=%fused_computation.7.clone.1 | convolution fusion | flops 2189426176 | bytes 4397568 | tf_op jit(solution)/shard_map/while/body/eval_jaxpr/rk,ck->rc/dot_general | solution.py:35
  179.7 0.1 dynamic_update_slice.6
  179.8 10.4 %select_reduce_fusion.7 = f32[512]{0:T(512)S(1)} fusion(bf16[16384,128]{1,0:T(8,128)(2,1)} %get-tuple-element.160, s32[16384]{0:T(1024)S(1)} %get-tuple-element.157, s32[512]{0:T(512)S(1)} %bitcast.43, s32[512]{0:T(512)S(1)} %bitcast.42, bf16[4,512,128]{2,1,0:T(8,128)(2,1)} %get-tuple-element.159, s32[]{:T(128)} %get-tuple-element.145), kind=kOutput, calls=%fused_computation.7.clone.1 | convolution fusion | flops 2189426176 | bytes 4397568 | tf_op jit(solution)/shard_map/while/body/eval_jaxpr/rk,ck->rc/dot_general | solution.py:35
  190.1 0.1 dynamic_update_slice.6
  190.2 23.0 %gather_fusion = f32[4096]{0:T(1024)S(1)} fusion(f32[2048]{0:T(1024)S(1)} %bitcast.35, s32[4096]{0:T(1024)S(1)} %broadcast_clamp_fusion), kind=kCustom, calls=%fused_computation | custom fusion | bytes 49152 | tf_op jit(solution)/shard_map/gather | solution.py:118
  213.2 0.1 all_to_all.18
  213.3 16.1 %all_to_all.23 = f32[128,1,32]{2,1,0:T(1,128)S(1)} all-to-all(f32[128,1,32]{2,1,0:T(1,128)S(1)} %bitcast.38), channel_id=1, replica_groups=mesh['dp'=16,'narrow'=8] {'dp','narrow'}, dimensions={0} | all-to-all | bytes 32768 | tf_op jit(solution)/shard_map/all_to_all | solution.py:119
  229.5 0.5 broadcast.158
  230.0 0.8 reduce.7
  230.8 0.1 reshape.142
  230.9 20.5 %gather_fusion.1 = f32[2048]{0:T(1024)} fusion(f32[4096]{0:T(1024)S(1)} %reshape.142, s32[2048]{0:T(1024)S(1)} %get-tuple-element.81), kind=kCustom, calls=%fused_computation.1 | custom fusion | bytes 24576 | tf_op jit(solution)/shard_map/gather | solution.py:122
  (22 shorter events, 0.2 us)
Async XLA Ops:
  6.5 25.8 %copy-start = (bf16[2048,128]{1,0:T(8,128)(2,1)S(1)}, bf16[2048,128]{1,0:T(8,128)(2,1)}, u32[]{:S(2)}) copy-start(bf16[2048,128]{1,0:T(8,128)(2,1)} %param.7) | copy-start | bytes 1572868
  20.8 21.4 %all-to-all-start = ((s32[128,1,32]{2,1,0:T(1,128)}), s32[128,1,32]{2,1,0:T(1,128)S(1)}, u32[]{:S(2)}, u32[]{:S(2)}) async-start(s32[128,1,32]{2,1,0:T(1,128)} %bitcast.4), calls=%async_computation | async-start | bytes 131072 | tf_op jit(solution)/shard_map/all_to_all | solution.py:90
  42.2 27.6 %all-to-all-start.1 = ((bf16[128,32,128]{2,1,0:T(8,128)(2,1)}), bf16[128,32,128]{2,1,0:T(8,128)(2,1)S(1)}, u32[]{:S(2)}, u32[]{:S(2)}) async-start(bf16[128,32,128]{2,1,0:T(8,128)(2,1)} %bitcast.6), calls=%async_computation.1 | async-start | bytes 2097152 | tf_op jit(solution)/shard_map/all_to_all | solution.py:83
  50.3 98.1 %all-gather.2.cloned.1.call-start = ((), (), s32[]{:S(2)}) async-start(), calls=%async_computation.3 | async-start | bytes 4718592 | tf_op jit(solution)/shard_map/all_gather | solution.py:113
Sparse Core Ops, SparseCore 0:
  81.5 66.8 all-gather.1
where the time goes:
time: 259 us; the launch traced here: 258 us
  waiting for transfers between devices  84.6 us (33%)
  local copies, waits for them, and re-layouts  65.9 us (25%)
  matrix products  41.4 us (16%)
  starting transfers between devices  19.6 us (8%)
  other arithmetic  16.9 us (7%)
  blocking collectives  16.1 us (6%)
  between operations  13.6 us (5%)
    all_gather x1, waiting for transfers between devices, shards(): lax.all_gather(local_rows, 'narrow', axis=0, tiled=True)  64.9 us
    dot_general x4, matrix products, per_block(): jnp.einsum('rk,ck->rc', row_block, column_piece, preferred_element_type=j...  41.4 us
    gather x1, local copies, waits for them, and re-layouts, shards(): answer = best_score[jnp.minimum(in_slot, rows_dev - 1)]  23 us
    gather x1, local copies, waits for them, and re-layouts, shards(): return returned.reshape(-1)[flat_index]  20.5 us
    all_to_all x1, waiting for transfers between devices, shards(): lax.all_to_all(outgoing.reshape(devices, capacity, features), ('dp', 'nar...  18 us
    all_to_all x1, blocking collectives, shards(): lax.all_to_all(answer.reshape(devices, capacity), ('dp', 'narrow'), split...  16.1 us
    scatter x1, local copies, waits for them, and re-layouts, shards(): jnp.zeros((rows_dev, features), jnp.bfloat16).at[in_slot]  11.6 us
    all_to_all x1, starting transfers between devices, shards(): lax.all_to_all(out_slot.reshape(devices, capacity), ('dp', 'narrow'), spl...  11.5 us
  transfers between devices with their start and end apart: 3, of which 3 were waited for; matrix products, arithmetic and copies ran while one was open for 5% of the time, Pallas kernels for 0%

commit v1 on v0

v1 whole, which is shorter than its diff:
```python
import jax
import jax.numpy as jnp
from jax import lax
from jax.experimental import pallas as pl
from jax.experimental.pallas import tpu as pltpu
from jax.sharding import PartitionSpec as P

MESH = pl.DeviceIdType.MESH
NT = (((1,), (1,)), ((), ()))
DEV = 128
CAP = 32
ROWS = 2048
EMB = 128
CHUNKS = 4
CROWS = ROWS // CHUNKS
BF = jnp.bfloat16
F32 = jnp.float32
I32 = jnp.int32


def div(a, b):
    return lax.div(a, jnp.int32(b))


def rem(a, b):
    return lax.rem(a, jnp.int32(b))


def place(x, y, z, core):
    return (y * 4 + rem(x, 2) * 2 + core, z * 2 + div(x, 2))


def place_of(index):
    member = rem(index, 8)
    group = div(index, 8)
    return place(rem(group, 4), div(group, 4), div(member, 2), rem(member, 2))


def split3(value):
    high = value.astype(BF)
    rest = value - high.astype(F32)
    middle = rest.astype(BF)
    low = (rest - middle.astype(F32)).astype(BF)
    return jnp.concatenate([high, middle, low], axis=0)


def kernel(
    emb_ref, cid_ref, rank_ref, size_ref, owner_ref, out_ref,
    normed, bucket, arrived, slot_out, slot_in, dest_hot, dest_row, pos_row, flat_row,
    total, blocks, row_feat, col_feat, best, part_out, part_in, table, answer, answer_in, turned,
    send_slot, recv_slot, send_row, recv_row, send_block, recv_block, send_part, recv_part, send_ans, recv_ans,
):
    dp = lax.axis_index("dp")
    nar = lax.axis_index("narrow")
    y, core = div(dp, 4), rem(dp, 2)
    x = rem(nar, 2) * 2 + rem(div(dp, 2), 2)
    z = div(nar, 2)
    group = y * 4 + x
    member = z * 2 + core
    me = group * 8 + member
    quarter = rem(me, 4) * CAP

    barrier = pltpu.get_barrier_semaphore()

    def greet(i, carry):
        pl.semaphore_signal(barrier, inc=1, device_id=place_of(rem(me + i, DEV)), device_id_type=MESH)
        return carry

    lax.fori_loop(1, DEV, greet, 0)

    cid = cid_ref[...]

    def owners(j, carry):
        owner, bound, seen = carry
        own = owner_ref[j]
        owner = jnp.where(cid == j, own, owner)
        mine = own == group
        bound = jnp.where(mine & (seen == 0), size_ref[j], bound)
        seen = jnp.where(mine, 1, seen)
        return owner, bound, seen

    owner, bound, _ = lax.fori_loop(
        0, 32, owners, (jnp.zeros((1, ROWS), I32), jnp.int32(0), jnp.int32(0))
    )

    def offsets(j, offset):
        return offset + jnp.where((owner == owner_ref[j]) & (cid > j), size_ref[j], 0)

    offset = lax.fori_loop(0, 32, offsets, rank_ref[...])
    dest = owner * 8 + (offset >> 11)
    local = offset & (ROWS - 1)
    dest_row[...] = dest

    hot = dest == lax.broadcasted_iota(I32, (DEV, ROWS), 0)
    dest_hot[...] = jnp.where(hot, 1.0, 0.0).astype(BF)
    upper = jnp.where(
        lax.broadcasted_iota(I32, (256, 256), 0) <= lax.broadcasted_iota(I32, (256, 256), 1), 1.0, 0.0
    ).astype(BF)
    before = jnp.full((DEV, 1), -1.0, F32)
    for k in range(ROWS // 256):
        piece = dest_hot[:, k * 256:(k + 1) * 256]
        count = jnp.dot(piece, upper, preferred_element_type=F32)
        position = jnp.sum(jnp.where(piece.astype(F32) > 0.5, count + before, 0.0), axis=0, keepdims=True)
        pos_row[:, k * 256:(k + 1) * 256] = position.astype(I32)
        before = before + count[:, 255:256]
    pos = pos_row[...]
    flat_row[...] = dest * CAP + pos

    lane_hot = (pos + quarter) == lax.broadcasted_iota(I32, (DEV, ROWS), 0)
    code = local + 1
    high = jnp.where(lane_hot, (code & ~63).astype(F32), 0.0).astype(BF)
    low = jnp.where(lane_hot, (code & 63).astype(F32), 0.0).astype(BF)
    codes = lax.dot_general(dest_hot[...], high, NT, preferred_element_type=F32)
    codes = codes + lax.dot_general(dest_hot[...], low, NT, preferred_element_type=F32)
    slot_out[...] = codes.astype(I32).reshape(DEV, 1, 128)

    pl.semaphore_wait(barrier, DEV - 1)

    def send_slots(i, carry):
        to = rem(me + i, DEV)
        pltpu.make_async_remote_copy(
            src_ref=slot_out.at[to], dst_ref=slot_in.at[me], send_sem=send_slot, recv_sem=recv_slot,
            device_id=place_of(to), device_id_type=MESH,
        ).start()
        return carry

    lax.fori_loop(1, DEV, send_slots, 0)
    pltpu.make_async_copy(slot_out.at[me], slot_in.at[me], recv_slot).start()

    wide = emb_ref[...].astype(F32)
    normed[...] = (wide * lax.rsqrt(jnp.sum(wide * wide, axis=1, keepdims=True) + 1e-06)).astype(BF)

    flip_x = 1 - 2 * rem(x, 2)
    flip_y = 1 - 2 * rem(y, 2)

    def partner(i):
        px = rem(x + flip_x * rem(i, 4) + 4, 4)
        py = rem(y + flip_y * div(i, 4) + 4, 4)
        return py * 4 + px

    def fill(other):
        wanted = other * 256 + lax.broadcasted_iota(I32, (256, ROWS), 0)
        pick = jnp.where(flat_row[...] == wanted, 1.0, 0.0).astype(BF)
        rows = jnp.dot(pick, normed[...], preferred_element_type=F32)
        bucket[pl.ds(pl.multiple_of(other * 256, 256), 256), :] = rows.astype(BF)

    def send_rows(other, j):
        to = other * 8 + rem(member + j, 8)
        pltpu.make_async_remote_copy(
            src_ref=bucket.at[pl.ds(pl.multiple_of(to * CAP, CAP), CAP)],
            dst_ref=arrived.at[pl.ds(pl.multiple_of(me * CAP, CAP), CAP)],
            send_sem=send_row, recv_sem=recv_row.at[group],
            device_id=place_of(to), device_id_type=MESH,
        ).start()

    def dispatch(i, carry):
        other = partner(i)
        fill(other)
        for j in range(8):
            send_rows(other, j)
        return carry

    lax.fori_loop(1, 16, dispatch, 0)
    fill(group)
    for j in range(1, 8):
        send_rows(group, j)
    mine = pl.ds(pl.multiple_of(me * CAP, CAP), CAP)
    pltpu.make_async_copy(bucket.at[mine], arrived.at[mine], recv_row.at[group]).start()

    up = rem(z + 1, 4)
    down = rem(z + 3, 4)
    first_lane = lax.broadcasted_iota(I32, (256, EMB), 1) == 0
    numbers = (member, up * 2 + core, down * 2 + core, up * 2 + 1 - core)
    for b in range(4):
        def features(t, carry):
            at = pl.ds(pl.multiple_of(t * 256, 256), 256)
            slot = numbers[b] * ROWS + t * 256 + lax.broadcasted_iota(I32, (256, EMB), 0)
            late = slot >= bound
            row_feat[b, at, :] = jnp.where(first_lane & late, 1.0, 0.0).astype(BF)
            col_feat[b, at, :] = jnp.where(first_lane & jnp.logical_not(late), -8.0, 0.0).astype(BF)
            return carry

        lax.fori_loop(0, 8, features, 0)
    best[...] = jnp.full((4, 8, ROWS), -1.0, F32)

    total[...] = jnp.zeros((ROWS, EMB), F32)
    pltpu.make_async_copy(slot_in, slot_in, recv_slot).wait()

    def codes_of(k):
        return jnp.sum(slot_in[pl.ds(4 * k, 4)], axis=0)

    def compact(i, carry):
        other = partner(rem(i, 16))
        at = pl.ds(pl.multiple_of(other * 256, 256), 256)
        pltpu.make_async_copy(arrived.at[at], arrived.at[at], recv_row.at[other]).wait()
        code_row = jnp.concatenate([codes_of(2 * other), codes_of(2 * other + 1)], axis=1)
        rows = arrived[at, :]
        for m in range(4):
            wanted = lax.broadcasted_iota(I32, (512, 256), 0) + (m * 512 + 1)
            pick = jnp.where(code_row == wanted, 1.0, 0.0).astype(BF)
            total[m * 512:(m + 1) * 512, :] += jnp.dot(pick, rows, preferred_element_type=F32)
        return carry

    lax.fori_loop(1, 17, compact, 0)
    blocks[0] = total[...].astype(BF)

    def block_copy(src, dst, ch, to):
        rows = pl.ds(ch * CROWS, CROWS)
        return pltpu.make_async_remote_copy(
            src_ref=blocks.at[src, rows], dst_ref=blocks.at[dst, rows],
            send_sem=send_block.at[dst], recv_sem=recv_block.at[dst, ch],
            device_id=to, device_id_type=MESH,
        )

    above = place(x, y, up, core)
    below = place(x, y, down, core)
    beside = place(x, y, z, 1 - core)
    above_beside = place(x, y, up, 1 - core)
    for ch in range(CHUNKS):
        block_copy(0, 1, ch, below).start()
        block_copy(0, 2, ch, above).start()

    def tile(row_block, rt, col_block, ct, diagonal):
        rat = pl.ds(pl.multiple_of(rt * 256, 256), 256)
        width = 256 if diagonal else 512
        cat = pl.ds(pl.multiple_of(ct * width, width), width)
        rows = jnp.concatenate([blocks[row_block, rat, :], row_feat[row_block, rat, :]], axis=1)
        cols = jnp.concatenate([blocks[col_block, cat, :], col_feat[col_block, cat, :]], axis=1)
        scores = lax.dot_general(cols, rows, NT, preferred_element_type=F32)
        if diagonal:
            c = lax.broadcasted_iota(I32, (width, 256), 0) + ct * 256
            r = lax.broadcasted_iota(I32, (width, 256), 1) + rt * 256
            scores = jnp.where(c < r, scores, -1.0)
        top = jnp.max(scores.reshape(width // 8, 8, 256), axis=0)
        best[row_block, :, rat] = jnp.maximum(best[row_block, :, rat], top)

    def triangle(rt, carry):
        def inner(ct, carry):
            tile(0, rt, 0, ct, True)
            return carry

        return lax.fori_loop(0, rt + 1, inner, carry)

    lax.fori_loop(0, 8, triangle, 0)

    def later(p, q):
        return jnp.where(numbers[q] > numbers[p], 1, 0)

    def pair_chunk(p, q, ch):
        flag = later(p, q)
        row_block = flag * q + (1 - flag) * p
        col_block = flag * p + (1 - flag) * q

        def unit(u, carry):
            rt = flag * (ch * 2 + rem(u, 2)) + (1 - flag) * u
            ct = flag * div(u, 2) + (1 - flag) * ch
            tile(row_block, rt, col_block, ct, False)
            return carry

        lax.fori_loop(0, 8, unit, 0)

    def pair_half(p, q, half):
        flag = later(p, q)
        row_block = flag * q + (1 - flag) * p
        col_block = flag * p + (1 - flag) * q

        def unit(u, carry):
            tile(row_block, div(u, 2), col_block, half * 2 + rem(u, 2), False)
            return carry

        lax.fori_loop(0, 16, unit, 0)

    for ch in range(CHUNKS):
        block_copy(0, 1, ch, below).wait_recv()
        block_copy(1, 3, ch, beside).start()
        pair_chunk(0, 1, ch)
    for ch in range(CHUNKS):
        block_copy(0, 2, ch, above).wait_recv()
    pair_half(1, 2, div(z, 2))
    for ch in range(CHUNKS):
        block_copy(1, 3, ch, beside).wait_recv()
        pair_chunk(0, 3, ch)
    pair_half(1, 3, core)
    pair_half(2, 3, core)

    whole = blocks.at[0]
    for dst in (1, 2, 3):
        part_out[dst] = jnp.max(best[dst], axis=0, keepdims=True)
        pltpu.make_async_remote_copy(
            src_ref=part_out.at[dst], dst_ref=part_in.at[dst], send_sem=send_part.at[dst], recv_sem=recv_part.at[dst],
            device_id=(None, above, below, above_beside)[dst], device_id_type=MESH,
        ).start()
    top = jnp.max(best[0], axis=0, keepdims=True)
    for dst in (1, 2, 3):
        pltpu.make_async_copy(part_in.at[dst], part_in.at[dst], recv_part.at[dst]).wait()
        top = jnp.maximum(top, part_in[dst])

    for k in range(16):
        table[k:k + 1, :] = top[:, k * 128:(k + 1) * 128]
    values = split3(table[...])
    for part in range(4):
        index = jnp.concatenate([codes_of(part * 8 + k) for k in range(8)], axis=1) - 1
        fine = jnp.where((index & 127) == lax.broadcasted_iota(I32, (128, 1024), 0), 1.0, 0.0).astype(BF)
        found = jnp.dot(values, fine, preferred_element_type=F32)
        found = (found[0:16] + found[16:32]) + found[32:48]
        coarse = (index >> 7) == lax.broadcasted_iota(I32, (16, 1024), 0)
        line = jnp.sum(jnp.where(coarse, found, 0.0), axis=0, keepdims=True)
        for k in range(8):
            answer[part * 8 + k] = line[:, k * 128:(k + 1) * 128]

    def send_answers(i, carry):
        to = rem(me + i, DEV)
        pltpu.make_async_remote_copy(
            src_ref=answer.at[div(to, 4)], dst_ref=answer_in.at[me], send_sem=send_ans, recv_sem=recv_ans,
            device_id=place_of(to), device_id_type=MESH,
        ).start()
        return carry

    lax.fori_loop(1, DEV, send_answers, 0)
    pltpu.make_async_copy(answer.at[div(me, 4)], answer_in.at[me], recv_ans).start()
    pltpu.make_async_copy(answer_in, answer_in, recv_ans).wait()

    turned[...] = answer_in[...].reshape(DEV, 128).T
    mine_back = split3(turned[pl.ds(pl.multiple_of(quarter, CAP), CAP), :])
    back = jnp.dot(mine_back, dest_hot[...], preferred_element_type=F32)
    back = (back[0:32] + back[32:64]) + back[64:96]
    spot = pos_row[...] == lax.broadcasted_iota(I32, (CAP, ROWS), 0)
    out_ref[...] = jnp.sum(jnp.where(spot, back, 0.0), axis=0, keepdims=True)

    others = pl.ds(0, DEV - 1)
    pltpu.make_async_copy(slot_in.at[others], slot_in.at[others], send_slot).wait()
    pltpu.make_async_copy(answer_in.at[others], answer_in.at[others], send_ans).wait()
    sent = pl.ds(0, (DEV - 1) * CAP)
    pltpu.make_async_copy(arrived.at[sent], arrived.at[sent], send_row).wait()
    for dst in (1, 2, 3):
        pltpu.make_async_copy(whole, whole, send_block.at[dst]).wait()
        pltpu.make_async_copy(part_in.at[dst], part_in.at[dst], send_part.at[dst]).wait()


def shards(embeddings, cluster_id, member_rank, cluster_size, cluster_owner):
    vmem = pl.BlockSpec(memory_space=pltpu.VMEM)
    smem = pl.BlockSpec(memory_space=pltpu.SMEM)
    dma = pltpu.SemaphoreType.DMA
    result = pl.pallas_call(
        kernel,
        out_shape=jax.ShapeDtypeStruct((1, ROWS), F32),
        in_specs=[vmem, vmem, vmem, smem, smem],
        out_specs=vmem,
        scratch_shapes=[
            pltpu.VMEM((ROWS, EMB), BF),
            pltpu.VMEM((DEV * CAP, EMB), BF),
            pltpu.VMEM((DEV * CAP, EMB), BF),
            pltpu.VMEM((DEV, 1, 128), I32),
            pltpu.VMEM((DEV, 1, 128), I32),
            pltpu.VMEM((DEV, ROWS), BF),
            pltpu.VMEM((1, ROWS), I32),
            pltpu.VMEM((1, ROWS), I32),
            pltpu.VMEM((1, ROWS), I32),
            pltpu.VMEM((ROWS, EMB), F32),
            pltpu.VMEM((4, ROWS, EMB), BF),
            pltpu.VMEM((4, ROWS, EMB), BF),
            pltpu.VMEM((4, ROWS, EMB), BF),
            pltpu.VMEM((4, 8, ROWS), F32),
            pltpu.VMEM((4, 1, ROWS), F32),
            pltpu.VMEM((4, 1, ROWS), F32),
            pltpu.VMEM((16, 128), F32),
            pltpu.VMEM((32, 1, 128), F32),
            pltpu.VMEM((DEV, 1, 128), F32),
            pltpu.VMEM((128, DEV), F32),
            dma, dma, dma, dma((16,)), dma((4,)), dma((4, CHUNKS)), dma((4,)), dma((4,)), dma, dma,
        ],
        compiler_params=pltpu.CompilerParams(
            collective_id=0, has_side_effects=True, vmem_limit_bytes=48 * 1024 * 1024
        ),
        cost_estimate=pl.CostEstimate(flops=12 * 10**9, bytes_accessed=1 << 20, transcendentals=2048),
    )(embeddings, cluster_id.reshape(1, ROWS), member_rank.reshape(1, ROWS), cluster_size, cluster_owner)
    return result.reshape(ROWS)


def solution(mesh):
    in_specs = (P(("dp", "narrow"), None), P(("dp", "narrow")), P(("dp", "narrow")), P(), P())
    out_specs = P(("dp", "narrow"))
    return jax.shard_map(shards, mesh=mesh, in_specs=in_specs, out_specs=out_specs, check_vma=False)
```

time: 259 us -> 95.2 us (0.37)
  Pallas kernels: 0 us -> 91.3 us
  waiting for transfers between devices: 84.6 us -> 0 us
  local copies, waits for them, and re-layouts: 65.9 us -> 3.7 us
  matrix products: 41.4 us -> 0 us
  starting transfers between devices: 19.6 us -> 0 us
  other arithmetic: 16.9 us -> 0 us
  blocking collectives: 16.1 us -> 0 us
  between operations: 13.6 us -> 0.01 us
    pallas_call x0 -> x1, Pallas kernels: none -> 91.3 us  [shards(): pl.pallas_call(kernel, out_shape=jax.ShapeDtypeStruct((1, ROWS), F32), in...]
    all_gather x1 -> x0, waiting for transfers between devices: 64.9 us -> none  [shards(): lax.all_gather(local_rows, 'narrow', axis=0, tiled=True)]
    gather x2 -> x0, local copies, waits for them, and re-layouts: 43.6 us -> none  [the longest x1 23 us: shards(): answer = best_score[jnp.minimum(in_slot, rows_dev - 1)]]
    dot_general x4 -> x0, matrix products: 41.4 us -> none  [per_block(): jnp.einsum('rk,ck->rc', row_block, column_piece, preferred_element_type=j...]
    all_to_all x2 -> x0, waiting for transfers between devices: 19.7 us -> none  [the longest x1 18 us: shards(): lax.all_to_all(outgoing.reshape(devices, capacity, features), ('dp', 'nar...]
    scatter x2 -> x0, local copies, waits for them, and re-layouts: 19.6 us -> none  [the longest x1 11.6 us: shards(): jnp.zeros((rows_dev, features), jnp.bfloat16).at[in_slot]]
    all_to_all x2 -> x0, starting transfers between devices: 19.5 us -> none  [the longest x1 11.5 us: shards(): lax.all_to_all(out_slot.reshape(devices, capacity), ('dp', 'narrow'), spl...]
    all_to_all x1 -> x0, blocking collectives: 16.1 us -> none  [shards(): lax.all_to_all(answer.reshape(devices, capacity), ('dp', 'narrow'), split...]
  transfers between devices with their start and end apart: 3 -> 0, of which waited for: 3 -> 0; matrix products, arithmetic and copies ran while one was open for 5% -> 0% of each run, Pallas kernels for 0% -> 0%
where the time goes in v1:
time: 95.2 us; the launch traced here: 95 us
  Pallas kernels  91.3 us (96%)
  local copies, waits for them, and re-layouts  3.7 us (4%)
    pallas_call x1, Pallas kernels, shards(): pl.pallas_call(kernel, out_shape=jax.ShapeDtypeStruct((1, ROWS), F32), in...  91.3 us
    unnamed x11, local copies, waits for them, and re-layouts  3.7 us

profile of v1, /device:TPU:1, one launch (start us, length us, event | category | flops | bytes accessed | tf_op | source)
XLA Modules:
  0.0 95.0 jit_solution(15792879959323436535)
XLA Ops:
  0.0 0.0 copy-start.3
  0.0 0.0 copy-start.4
  0.0 0.7 copy-done.3
  0.7 0.0 copy-done.4
  0.7 0.0 copy-start
  0.7 1.0 %copy-done = bf16[2048,128]{1,0:T(8,128)(2,1)S(1)} copy-done((bf16[2048,128]{1,0:T(8,128)(2,1)S(1)}, bf16[2048,128]{1,0:T(8,128)(2,1)}, u32[]{:S(2)}) %copy-start) | copy-done | bytes 524312
  1.7 0.0 copy-start.1
  1.7 0.7 copy-done.1
  2.4 0.0 copy-start.2
  2.4 0.7 copy-done.2
  3.1 91.3 %shard_map.55 = f32[1,2048]{1,0:T(1,128)S(1)} custom-call(bf16[2048,128]{1,0:T(8,128)(2,1)S(1)} %copy-done, s32[1,2048]{1,0:T(1,128)S(1)} %bitcast.4, s32[1,2048]{1,0:T(1,128)S(1)} %bitcast.5, s32[32]{0:T(128)S(1)} %copy-done.3, s32[32]{0:T(128)S(1)} %copy-done.4), custom_call_target="tpu_custom_call" | custom-call | flops 12000000000 | bytes 1048576 | tf_op jit(solution)/shard_map/pallas_call | solution.py:344
  94.4 0.6 copy.7
Async XLA Ops:
  0.0 0.7 copy-start.3
  0.0 0.7 copy-start.4
  0.7 1.0 %copy-start = (bf16[2048,128]{1,0:T(8,128)(2,1)S(1)}, bf16[2048,128]{1,0:T(8,128)(2,1)}, u32[]{:S(2)}) copy-start(bf16[2048,128]{1,0:T(8,128)(2,1)} %emb_ref.1) | copy-start | bytes 1572868
  1.7 0.7 copy-start.1
  2.4 0.7 copy-start.2

commit v2 on v1

--- a/solution.py
+++ b/solution.py
@@ -30,12 +30,6 @@
     return (y * 4 + rem(x, 2) * 2 + core, z * 2 + div(x, 2))
 
 
-def place_of(index):
-    member = rem(index, 8)
-    group = div(index, 8)
-    return place(rem(group, 4), div(group, 4), div(member, 2), rem(member, 2))
-
-
 def split3(value):
     high = value.astype(BF)
     rest = value - high.astype(F32)
@@ -45,7 +39,8 @@
 
 
 def kernel(
-    emb_ref, cid_ref, rank_ref, size_ref, owner_ref, out_ref,
+    emb_hbm, cid_hbm, rank_hbm, size_hbm, owner_hbm, out_ref,
+    emb_ref, cid_ref, rank_ref, size_ref, owner_ref, load_sem,
     normed, bucket, arrived, slot_out, slot_in, dest_hot, dest_row, pos_row, flat_row,
     total, blocks, row_feat, col_feat, best, part_out, part_in, table, answer, answer_in, turned,
     send_slot, recv_slot, send_row, recv_row, send_block, recv_block, send_part, recv_part, send_ans, recv_ans,
@@ -57,16 +52,37 @@
     z = div(nar, 2)
     group = y * 4 + x
     member = z * 2 + core
-    me = group * 8 + member
+    me = dp * 8 + nar
     quarter = rem(me, 4) * CAP
 
+    loads = [
+        pltpu.make_async_copy(src, dst, load_sem.at[k])
+        for k, (src, dst) in enumerate(
+            ((owner_hbm, owner_ref), (size_hbm, size_ref), (cid_hbm, cid_ref), (rank_hbm, rank_ref), (emb_hbm, emb_ref))
+        )
+    ]
+    for load in loads:
+        load.start()
+
     barrier = pltpu.get_barrier_semaphore()
 
-    def greet(i, carry):
-        pl.semaphore_signal(barrier, inc=1, device_id=place_of(rem(me + i, DEV)), device_id_type=MESH)
-        return carry
-
-    lax.fori_loop(1, DEV, greet, 0)
+    def to_all(act):
+        def line(i, carry):
+            other = rem(dp + i, 16)
+            for j in range(8):
+                act(other, rem(nar + j, 8))
+            return carry
+
+        lax.fori_loop(1, 16, line, 0)
+        for j in range(1, 8):
+            act(dp, rem(nar + j, 8))
+
+    def greet(other, column):
+        pl.semaphore_signal(barrier, inc=1, device_id=(other, column), device_id_type=MESH)
+
+    to_all(greet)
+    for load in loads:
+        load.wait()
 
     cid = cid_ref[...]
 
@@ -87,7 +103,10 @@
         return offset + jnp.where((owner == owner_ref[j]) & (cid > j), size_ref[j], 0)
 
     offset = lax.fori_loop(0, 32, offsets, rank_ref[...])
-    dest = owner * 8 + (offset >> 11)
+    seat = offset >> 11
+    dest = (
+        ((owner >> 2) << 5) + ((owner & 1) << 4) + ((seat & 1) << 3) + ((seat >> 1) << 1) + ((owner >> 1) & 1)
+    )
     local = offset & (ROWS - 1)
     dest_row[...] = dest
 
@@ -116,27 +135,16 @@
 
     pl.semaphore_wait(barrier, DEV - 1)
 
-    def send_slots(i, carry):
-        to = rem(me + i, DEV)
-        pltpu.make_async_remote_copy(
-            src_ref=slot_out.at[to], dst_ref=slot_in.at[me], send_sem=send_slot, recv_sem=recv_slot,
-            device_id=place_of(to), device_id_type=MESH,
-        ).start()
-        return carry
-
-    lax.fori_loop(1, DEV, send_slots, 0)
-    pltpu.make_async_copy(slot_out.at[me], slot_in.at[me], recv_slot).start()
-
     wide = emb_ref[...].astype(F32)
     normed[...] = (wide * lax.rsqrt(jnp.sum(wide * wide, axis=1, keepdims=True) + 1e-06)).astype(BF)
 
-    flip_x = 1 - 2 * rem(x, 2)
     flip_y = 1 - 2 * rem(y, 2)
+    half_x = rem(x, 2)
 
     def partner(i):
-        px = rem(x + flip_x * rem(i, 4) + 4, 4)
-        py = rem(y + flip_y * div(i, 4) + 4, 4)
-        return py * 4 + px
+        k = rem(i * 7, 16)
+        py = rem(y + flip_y * div(k, 4) + 4, 4)
+        return py * 4 + rem(half_x + div(k, 2), 2) * 2 + rem(core + k, 2)
 
     def fill(other):
         wanted = other * 256 + lax.broadcasted_iota(I32, (256, ROWS), 0)
@@ -145,12 +153,17 @@
         bucket[pl.ds(pl.multiple_of(other * 256, 256), 256), :] = rows.astype(BF)
 
     def send_rows(other, j):
-        to = other * 8 + rem(member + j, 8)
+        column = rem(nar + j, 8)
+        to = other * 8 + column
+        pltpu.make_async_remote_copy(
+            src_ref=slot_out.at[to], dst_ref=slot_in.at[me], send_sem=send_slot, recv_sem=recv_slot.at[dp],
+            device_id=(other, column), device_id_type=MESH,
+        ).start()
         pltpu.make_async_remote_copy(
             src_ref=bucket.at[pl.ds(pl.multiple_of(to * CAP, CAP), CAP)],
             dst_ref=arrived.at[pl.ds(pl.multiple_of(me * CAP, CAP), CAP)],
-            send_sem=send_row, recv_sem=recv_row.at[group],
-            device_id=place_of(to), device_id_type=MESH,
+            send_sem=send_row, recv_sem=recv_row.at[dp],
+            device_id=(other, column), device_id_type=MESH,
         ).start()
 
     def dispatch(i, carry):
@@ -161,11 +174,12 @@
         return carry
 
     lax.fori_loop(1, 16, dispatch, 0)
-    fill(group)
+    fill(dp)
     for j in range(1, 8):
-        send_rows(group, j)
+        send_rows(dp, j)
     mine = pl.ds(pl.multiple_of(me * CAP, CAP), CAP)
-    pltpu.make_async_copy(bucket.at[mine], arrived.at[mine], recv_row.at[group]).start()
+    pltpu.make_async_copy(slot_out.at[me], slot_in.at[me], recv_slot.at[dp]).start()
+    pltpu.make_async_copy(bucket.at[mine], arrived.at[mine], recv_row.at[dp]).start()
 
     up = rem(z + 1, 4)
     down = rem(z + 3, 4)
@@ -184,24 +198,29 @@
     best[...] = jnp.full((4, 8, ROWS), -1.0, F32)
 
     total[...] = jnp.zeros((ROWS, EMB), F32)
-    pltpu.make_async_copy(slot_in, slot_in, recv_slot).wait()
 
     def codes_of(k):
         return jnp.sum(slot_in[pl.ds(4 * k, 4)], axis=0)
 
     def compact(i, carry):
-        other = partner(rem(i, 16))
-        at = pl.ds(pl.multiple_of(other * 256, 256), 256)
-        pltpu.make_async_copy(arrived.at[at], arrived.at[at], recv_row.at[other]).wait()
-        code_row = jnp.concatenate([codes_of(2 * other), codes_of(2 * other + 1)], axis=1)
-        rows = arrived[at, :]
+        rows, codes = [], []
+        for k in range(2):
+            other = partner(rem(2 * i + 1 + k, 16))
+            at = pl.ds(pl.multiple_of(other * 256, 256), 256)
+            ats = pl.ds(pl.multiple_of(other * 8, 8), 8)
+            pltpu.make_async_copy(slot_in.at[ats], slot_in.at[ats], recv_slot.at[other]).wait()
+            pltpu.make_async_copy(arrived.at[at], arrived.at[at], recv_row.at[other]).wait()
+            codes += [codes_of(2 * other), codes_of(2 * other + 1)]
+            rows.append(arrived[at, :])
+        code_row = jnp.concatenate(codes, axis=1)
+        rows = jnp.concatenate(rows, axis=0)
         for m in range(4):
-            wanted = lax.broadcasted_iota(I32, (512, 256), 0) + (m * 512 + 1)
+            wanted = lax.broadcasted_iota(I32, (512, 512), 0) + (m * 512 + 1)
             pick = jnp.where(code_row == wanted, 1.0, 0.0).astype(BF)
             total[m * 512:(m + 1) * 512, :] += jnp.dot(pick, rows, preferred_element_type=F32)
         return carry
 
-    lax.fori_loop(1, 17, compact, 0)
+    lax.fori_loop(0, 8, compact, 0)
     blocks[0] = total[...].astype(BF)
 
     def block_copy(src, dst, ch, to):
@@ -308,15 +327,13 @@
         for k in range(8):
             answer[part * 8 + k] = line[:, k * 128:(k + 1) * 128]
 
-    def send_answers(i, carry):
-        to = rem(me + i, DEV)
+    def send_answer(other, column):
         pltpu.make_async_remote_copy(
-            src_ref=answer.at[div(to, 4)], dst_ref=answer_in.at[me], send_sem=send_ans, recv_sem=recv_ans,
-            device_id=place_of(to), device_id_type=MESH,
+            src_ref=answer.at[other * 2 + div(column, 4)], dst_ref=answer_in.at[me], send_sem=send_ans, recv_sem=recv_ans,
+            device_id=(other, column), device_id_type=MESH,
         ).start()
-        return carry
-
-    lax.fori_loop(1, DEV, send_answers, 0)
+
+    to_all(send_answer)
     pltpu.make_async_copy(answer.at[div(me, 4)], answer_in.at[me], recv_ans).start()
     pltpu.make_async_copy(answer_in, answer_in, recv_ans).wait()
 
@@ -339,14 +356,19 @@
 
 def shards(embeddings, cluster_id, member_rank, cluster_size, cluster_owner):
     vmem = pl.BlockSpec(memory_space=pltpu.VMEM)
-    smem = pl.BlockSpec(memory_space=pltpu.SMEM)
     dma = pltpu.SemaphoreType.DMA
     result = pl.pallas_call(
         kernel,
         out_shape=jax.ShapeDtypeStruct((1, ROWS), F32),
-        in_specs=[vmem, vmem, vmem, smem, smem],
+        in_specs=[pl.BlockSpec(memory_space=pltpu.HBM)] * 5,
         out_specs=vmem,
         scratch_shapes=[
+            pltpu.VMEM((ROWS, EMB), BF),
+            pltpu.VMEM((1, ROWS), I32),
+            pltpu.VMEM((1, ROWS), I32),
+            pltpu.SMEM((32,), I32),
+            pltpu.SMEM((32,), I32),
+            dma((5,)),
             pltpu.VMEM((ROWS, EMB), BF),
             pltpu.VMEM((DEV * CAP, EMB), BF),
             pltpu.VMEM((DEV * CAP, EMB), BF),
@@ -367,10 +389,10 @@
             pltpu.VMEM((32, 1, 128), F32),
             pltpu.VMEM((DEV, 1, 128), F32),
             pltpu.VMEM((128, DEV), F32),
-            dma, dma, dma, dma((16,)), dma((4,)), dma((4, CHUNKS)), dma((4,)), dma((4,)), dma, dma,
+            dma, dma((16,)), dma, dma((16,)), dma((4,)), dma((4, CHUNKS)), dma((4,)), dma((4,)), dma, dma,
         ],
         compiler_params=pltpu.CompilerParams(
-            collective_id=0, has_side_effects=True, vmem_limit_bytes=48 * 1024 * 1024
+            collective_id=0, has_side_effects=True, vmem_limit_bytes=62 * 1024 * 1024
         ),
         cost_estimate=pl.CostEstimate(flops=12 * 10**9, bytes_accessed=1 << 20, transcendentals=2048),
     )(embeddings, cluster_id.reshape(1, ROWS), member_rank.reshape(1, ROWS), cluster_size, cluster_owner)

time: 95.2 us -> 81 us (0.85)
  Pallas kernels: 91.3 us -> 79.6 us
  local copies, waits for them, and re-layouts: 3.7 us -> 1.3 us
    pallas_call x1, Pallas kernels: 91.3 us -> 79.6 us  [shards(): pl.pallas_call(kernel, out_shape=jax.ShapeDtypeStruct((1, ROWS), F32), in...]
    unnamed x11 -> x1, local copies, waits for them, and re-layouts: 3.7 us -> 1.3 us
where the time goes in v2:
time: 81 us; the launch traced here: 80.9 us
  Pallas kernels  79.6 us (98%)
  local copies, waits for them, and re-layouts  1.3 us (2%)
    pallas_call x1, Pallas kernels, shards(): pl.pallas_call(kernel, out_shape=jax.ShapeDtypeStruct((1, ROWS), F32), in...  79.6 us

profile of v2, /device:TPU:1, one launch (start us, length us, event | category | flops | bytes accessed | tf_op | source)
XLA Modules:
  0.0 80.9 jit_solution(5546623873781001316)
XLA Ops:
  0.0 79.6 %shard_map.55 = f32[1,2048]{1,0:T(1,128)} custom-call(bf16[2048,128]{1,0:T(8,128)(2,1)} %emb_hbm.1, s32[1,2048]{1,0:T(1,128)} %bitcast.4, s32[1,2048]{1,0:T(1,128)} %bitcast.5, s32[32]{0:T(128)} %size_hbm.1, s32[32]{0:T(128)} %owner_hbm.1), custom_call_target="tpu_custom_call" | custom-call | flops 12000000000 | bytes 1048576 | tf_op jit(solution)/shard_map/pallas_call | solution.py:360
  79.6 1.3 %copy.7 = f32[2048]{0:T(1024)} copy(f32[2048]{0:T(1024)} %bitcast.3) | data formatting | bytes 16384

commit v3 on v2

--- a/solution.py
+++ b/solution.py
@@ -133,10 +133,10 @@
     codes = codes + lax.dot_general(dest_hot[...], low, NT, preferred_element_type=F32)
     slot_out[...] = codes.astype(I32).reshape(DEV, 1, 128)
 
-    pl.semaphore_wait(barrier, DEV - 1)
-
     wide = emb_ref[...].astype(F32)
     normed[...] = (wide * lax.rsqrt(jnp.sum(wide * wide, axis=1, keepdims=True) + 1e-06)).astype(BF)
+
+    pl.semaphore_wait(barrier, DEV - 1)
 
     flip_y = 1 - 2 * rem(y, 2)
     half_x = rem(x, 2)
@@ -239,68 +239,69 @@
         block_copy(0, 1, ch, below).start()
         block_copy(0, 2, ch, above).start()
 
-    def tile(row_block, rt, col_block, ct, diagonal):
-        rat = pl.ds(pl.multiple_of(rt * 256, 256), 256)
-        width = 256 if diagonal else 512
-        cat = pl.ds(pl.multiple_of(ct * width, width), width)
-        rows = jnp.concatenate([blocks[row_block, rat, :], row_feat[row_block, rat, :]], axis=1)
-        cols = jnp.concatenate([blocks[col_block, cat, :], col_feat[col_block, cat, :]], axis=1)
-        scores = lax.dot_general(cols, rows, NT, preferred_element_type=F32)
-        if diagonal:
-            c = lax.broadcasted_iota(I32, (width, 256), 0) + ct * 256
-            r = lax.broadcasted_iota(I32, (width, 256), 1) + rt * 256
-            scores = jnp.where(c < r, scores, -1.0)
-        top = jnp.max(scores.reshape(width // 8, 8, 256), axis=0)
-        best[row_block, :, rat] = jnp.maximum(best[row_block, :, rat], top)
-
-    def triangle(rt, carry):
-        def inner(ct, carry):
-            tile(0, rt, 0, ct, True)
-            return carry
-
-        return lax.fori_loop(0, rt + 1, inner, carry)
-
-    lax.fori_loop(0, 8, triangle, 0)
-
-    def later(p, q):
-        return jnp.where(numbers[q] > numbers[p], 1, 0)
+    def score(row_block, row_at, col_block, col_at):
+        rows = jnp.concatenate([blocks[row_block, row_at, :], row_feat[row_block, row_at, :]], axis=1)
+        cols = jnp.concatenate([blocks[col_block, col_at, :], col_feat[col_block, col_at, :]], axis=1)
+        return lax.dot_general(cols, rows, NT, preferred_element_type=F32)
+
+    def fold(row_block, row_at, scores):
+        c, r = scores.shape
+        top = jnp.max(scores.reshape(c // 8, 8, r), axis=0)
+        best[row_block, :, row_at] = jnp.maximum(best[row_block, :, row_at], top)
+
+    for t in range(8):
+        at = pl.ds(t * 256, 256)
+        scores = score(0, at, 0, at)
+        c = lax.broadcasted_iota(I32, (256, 256), 0)
+        r = lax.broadcasted_iota(I32, (256, 256), 1)
+        fold(0, at, jnp.where(c < r, scores, -1.0))
+        if t:
+            fold(0, at, score(0, at, 0, pl.ds(0, t * 256)))
+
+    every = pl.ds(0, ROWS)
+
+    def either(condition, yes, no):
+        pl.when(condition)(yes)
+        pl.when(jnp.logical_not(condition))(no)
+
+    def meet(row_block, row_at, col_block, col_at):
+        fold(row_block, row_at, score(row_block, row_at, col_block, col_at))
 
     def pair_chunk(p, q, ch):
-        flag = later(p, q)
-        row_block = flag * q + (1 - flag) * p
-        col_block = flag * p + (1 - flag) * q
-
-        def unit(u, carry):
-            rt = flag * (ch * 2 + rem(u, 2)) + (1 - flag) * u
-            ct = flag * div(u, 2) + (1 - flag) * ch
-            tile(row_block, rt, col_block, ct, False)
-            return carry
-
-        lax.fori_loop(0, 8, unit, 0)
-
-    def pair_half(p, q, half):
-        flag = later(p, q)
-        row_block = flag * q + (1 - flag) * p
-        col_block = flag * p + (1 - flag) * q
-
-        def unit(u, carry):
-            tile(row_block, div(u, 2), col_block, half * 2 + rem(u, 2), False)
-            return carry
-
-        lax.fori_loop(0, 16, unit, 0)
+        at = pl.ds(ch * CROWS, CROWS)
+        either(
+            numbers[q] > numbers[p],
+            lambda: meet(q, at, p, every),
+            lambda: meet(p, every, q, at),
+        )
+
+    def pair_share(p, q, second, ch):
+        at = pl.ds(ch * CROWS, CROWS)
+        upto = pl.ds(0, (ch + 1) * CROWS)
+        under = pl.ds(0, ch * CROWS)
+
+        def roles(rows, cols):
+            def first():
+                meet(rows, upto, cols, at)
+
+            def other():
+                if ch:
+                    meet(rows, at, cols, under)
+
+            either(second == 0, first, other)
+
+        either(numbers[q] > numbers[p], lambda: roles(q, p), lambda: roles(p, q))
 
     for ch in range(CHUNKS):
         block_copy(0, 1, ch, below).wait_recv()
         block_copy(1, 3, ch, beside).start()
         pair_chunk(0, 1, ch)
-    for ch in range(CHUNKS):
         block_copy(0, 2, ch, above).wait_recv()
-    pair_half(1, 2, div(z, 2))
-    for ch in range(CHUNKS):
+        pair_share(1, 2, div(z, 2), ch)
         block_copy(1, 3, ch, beside).wait_recv()
         pair_chunk(0, 3, ch)
-    pair_half(1, 3, core)
-    pair_half(2, 3, core)
+        pair_share(1, 3, core, ch)
+        pair_share(2, 3, 1 - core, ch)
 
     whole = blocks.at[0]
     for dst in (1, 2, 3):

time: 81 us -> 60.2 us (0.74)
  Pallas kernels: 79.6 us -> 58.8 us
    pallas_call x1, Pallas kernels: 79.6 us -> 58.8 us  [shards(): pl.pallas_call(kernel, out_shape=jax.ShapeDtypeStruct((1, ROWS), F32), in...]
where the time goes in v3:
time: 60.2 us; the launch traced here: 60.1 us
  Pallas kernels  58.8 us (98%)
  local copies, waits for them, and re-layouts  1.3 us (2%)
    pallas_call x1, Pallas kernels, shards(): pl.pallas_call(kernel, out_shape=jax.ShapeDtypeStruct((1, ROWS), F32), in...  58.8 us
    unnamed x1, local copies, waits for them, and re-layouts  1.3 us

profile of v3, /device:TPU:1, one launch (start us, length us, event | category | flops | bytes accessed | tf_op | source)
XLA Modules:
  0.0 60.1 jit_solution(6793723727285453221)
XLA Ops:
  0.0 58.8 %shard_map.55 = f32[1,2048]{1,0:T(1,128)} custom-call(bf16[2048,128]{1,0:T(8,128)(2,1)} %emb_hbm.1, s32[1,2048]{1,0:T(1,128)} %bitcast.4, s32[1,2048]{1,0:T(1,128)} %bitcast.5, s32[32]{0:T(128)} %size_hbm.1, s32[32]{0:T(128)} %owner_hbm.1), custom_call_target="tpu_custom_call" | custom-call | flops 12000000000 | bytes 1048576 | tf_op jit(solution)/shard_map/pallas_call | solution.py:361
  58.8 1.3 %copy.7 = f32[2048]{0:T(1024)} copy(f32[2048]{0:T(1024)} %bitcast.3) | data formatting | bytes 16384

commit v4 on v3

--- a/solution.py
+++ b/solution.py
@@ -11,8 +11,8 @@
 CAP = 32
 ROWS = 2048
 EMB = 128
-CHUNKS = 4
-CROWS = ROWS // CHUNKS
+EDGES = (0, 512, 1024, 1536, 2048)
+CHUNKS = len(EDGES) - 1
 BF = jnp.bfloat16
 F32 = jnp.float32
 I32 = jnp.int32
@@ -42,7 +42,7 @@
     emb_hbm, cid_hbm, rank_hbm, size_hbm, owner_hbm, out_ref,
     emb_ref, cid_ref, rank_ref, size_ref, owner_ref, load_sem,
     normed, bucket, arrived, slot_out, slot_in, dest_hot, dest_row, pos_row, flat_row,
-    total, blocks, row_feat, col_feat, best, part_out, part_in, table, answer, answer_in, turned,
+    total, blocks, row_feat, col_feat, best, part_out, part_in, table, fine, coarse, answer, answer_in, turned,
     send_slot, recv_slot, send_row, recv_row, send_block, recv_block, send_part, recv_part, send_ans, recv_ans,
 ):
     dp = lax.axis_index("dp")
@@ -138,22 +138,19 @@
 
     pl.semaphore_wait(barrier, DEV - 1)
 
-    flip_y = 1 - 2 * rem(y, 2)
-    half_x = rem(x, 2)
-
-    def partner(i):
-        k = rem(i * 7, 16)
-        py = rem(y + flip_y * div(k, 4) + 4, 4)
-        return py * 4 + rem(half_x + div(k, 2), 2) * 2 + rem(core + k, 2)
+    total[...] = jnp.zeros((ROWS, EMB), F32)
+    def hot_rows(number, size):
+        number = jnp.where((number >= 0) & (number < size), number, -1).astype(F32).astype(BF)
+        count = lax.broadcasted_iota(I32, (size, number.shape[1]), 0).astype(F32).astype(BF)
+        return jnp.where(number == count, jnp.ones((), BF), jnp.zeros((), BF))
 
     def fill(other):
-        wanted = other * 256 + lax.broadcasted_iota(I32, (256, ROWS), 0)
-        pick = jnp.where(flat_row[...] == wanted, 1.0, 0.0).astype(BF)
+        pick = hot_rows(flat_row[...] - other * 256, 256)
         rows = jnp.dot(pick, normed[...], preferred_element_type=F32)
         bucket[pl.ds(pl.multiple_of(other * 256, 256), 256), :] = rows.astype(BF)
 
     def send_rows(other, j):
-        column = rem(nar + j, 8)
+        column = rem(nar + 3 * j % 8, 8)
         to = other * 8 + column
         pltpu.make_async_remote_copy(
             src_ref=slot_out.at[to], dst_ref=slot_in.at[me], send_sem=send_slot, recv_sem=recv_slot.at[dp],
@@ -167,22 +164,74 @@
         ).start()
 
     def dispatch(i, carry):
-        other = partner(i)
+        other = rem(dp + 5 * i, 16)
         fill(other)
         for j in range(8):
             send_rows(other, j)
         return carry
 
+
+    def codes_of(k):
+        return jnp.sum(slot_in[pl.ds(4 * k, 4)], axis=0)
+
+    def gather_in(i):
+        rows, codes = [], []
+        for k in range(2):
+            other = rem(dp + 80 - 5 * (2 * i + 1 + k), 16)
+            at = pl.ds(pl.multiple_of(other * 256, 256), 256)
+            ats = pl.ds(pl.multiple_of(other * 8, 8), 8)
+            pltpu.make_async_copy(slot_in.at[ats], slot_in.at[ats], recv_slot.at[other]).wait()
+            pltpu.make_async_copy(arrived.at[at], arrived.at[at], recv_row.at[other]).wait()
+            codes += [codes_of(2 * other), codes_of(2 * other + 1)]
+            rows.append(arrived[at, :])
+        return jnp.concatenate(codes, axis=1), jnp.concatenate(rows, axis=0)
+
+    def placed(ch, code_row, rows):
+        low, high = EDGES[ch], EDGES[ch + 1]
+        pick = jnp.concatenate([hot_rows(code_row - (first + 1), 256) for first in range(low, high, 256)], axis=0)
+        return total[low:high, :] + jnp.dot(pick, rows, preferred_element_type=F32)
+
+    def compact(i, carry):
+        code_row, rows = gather_in(i)
+        for ch in range(CHUNKS):
+            total[EDGES[ch]:EDGES[ch + 1], :] = placed(ch, code_row, rows)
+        return carry
+
+    def dispatch_own():
+        fill(dp)
+        for j in range(1, 8):
+            send_rows(dp, j)
+        mine = pl.ds(pl.multiple_of(me * CAP, CAP), CAP)
+        pltpu.make_async_copy(slot_out.at[me], slot_in.at[me], recv_slot.at[dp]).start()
+        pltpu.make_async_copy(bucket.at[mine], arrived.at[mine], recv_row.at[dp]).start()
+
     lax.fori_loop(1, 16, dispatch, 0)
-    fill(dp)
-    for j in range(1, 8):
-        send_rows(dp, j)
-    mine = pl.ds(pl.multiple_of(me * CAP, CAP), CAP)
-    pltpu.make_async_copy(slot_out.at[me], slot_in.at[me], recv_slot.at[dp]).start()
-    pltpu.make_async_copy(bucket.at[mine], arrived.at[mine], recv_row.at[dp]).start()
+    dispatch_own()
+    lax.fori_loop(0, 7, compact, 0)
+
+    def span(ch):
+        return pl.ds(EDGES[ch], EDGES[ch + 1] - EDGES[ch])
+
+    def block_copy(src, dst, ch, to):
+        rows = span(ch)
+        return pltpu.make_async_remote_copy(
+            src_ref=blocks.at[src, rows], dst_ref=blocks.at[dst, rows],
+            send_sem=send_block.at[dst], recv_sem=recv_block.at[dst, ch],
+            device_id=to, device_id_type=MESH,
+        )
 
     up = rem(z + 1, 4)
     down = rem(z + 3, 4)
+    above = place(x, y, up, core)
+    below = place(x, y, down, core)
+    beside = place(x, y, z, 1 - core)
+    above_beside = place(x, y, up, 1 - core)
+    code_row, rows = gather_in(7)
+    for ch in range(CHUNKS):
+        blocks[0, EDGES[ch]:EDGES[ch + 1], :] = placed(ch, code_row, rows).astype(BF)
+        block_copy(0, 1, ch, below).start()
+        block_copy(0, 2, ch, above).start()
+
     first_lane = lax.broadcasted_iota(I32, (256, EMB), 1) == 0
     numbers = (member, up * 2 + core, down * 2 + core, up * 2 + 1 - core)
     for b in range(4):
@@ -197,47 +246,11 @@
         lax.fori_loop(0, 8, features, 0)
     best[...] = jnp.full((4, 8, ROWS), -1.0, F32)
 
-    total[...] = jnp.zeros((ROWS, EMB), F32)
-
-    def codes_of(k):
-        return jnp.sum(slot_in[pl.ds(4 * k, 4)], axis=0)
-
-    def compact(i, carry):
-        rows, codes = [], []
-        for k in range(2):
-            other = partner(rem(2 * i + 1 + k, 16))
-            at = pl.ds(pl.multiple_of(other * 256, 256), 256)
-            ats = pl.ds(pl.multiple_of(other * 8, 8), 8)
-            pltpu.make_async_copy(slot_in.at[ats], slot_in.at[ats], recv_slot.at[other]).wait()
-            pltpu.make_async_copy(arrived.at[at], arrived.at[at], recv_row.at[other]).wait()
-            codes += [codes_of(2 * other), codes_of(2 * other + 1)]
-            rows.append(arrived[at, :])
-        code_row = jnp.concatenate(codes, axis=1)
-        rows = jnp.concatenate(rows, axis=0)
-        for m in range(4):
-            wanted = lax.broadcasted_iota(I32, (512, 512), 0) + (m * 512 + 1)
-            pick = jnp.where(code_row == wanted, 1.0, 0.0).astype(BF)
-            total[m * 512:(m + 1) * 512, :] += jnp.dot(pick, rows, preferred_element_type=F32)
-        return carry
-
-    lax.fori_loop(0, 8, compact, 0)
-    blocks[0] = total[...].astype(BF)
-
-    def block_copy(src, dst, ch, to):
-        rows = pl.ds(ch * CROWS, CROWS)
-        return pltpu.make_async_remote_copy(
-            src_ref=blocks.at[src, rows], dst_ref=blocks.at[dst, rows],
-            send_sem=send_block.at[dst], recv_sem=recv_block.at[dst, ch],
-            device_id=to, device_id_type=MESH,
-        )
-
-    above = place(x, y, up, core)
-    below = place(x, y, down, core)
-    beside = place(x, y, z, 1 - core)
-    above_beside = place(x, y, up, 1 - core)
-    for ch in range(CHUNKS):
-        block_copy(0, 1, ch, below).start()
-        block_copy(0, 2, ch, above).start()
+    for part in range(4):
+        index = jnp.concatenate([codes_of(part * 8 + k) for k in range(8)], axis=1) - 1
+        at = pl.ds(part * 1024, 1024)
+        fine[:, at] = jnp.where((index & 127) == lax.broadcasted_iota(I32, (128, 1024), 0), 1.0, 0.0).astype(BF)
+        coarse[:, at] = jnp.where((index >> 7) == lax.broadcasted_iota(I32, (16, 1024), 0), 1.0, 0.0)
 
     def score(row_block, row_at, col_block, col_at):
         rows = jnp.concatenate([blocks[row_block, row_at, :], row_feat[row_block, row_at, :]], axis=1)
@@ -268,7 +281,7 @@
         fold(row_block, row_at, score(row_block, row_at, col_block, col_at))
 
     def pair_chunk(p, q, ch):
-        at = pl.ds(ch * CROWS, CROWS)
+        at = span(ch)
         either(
             numbers[q] > numbers[p],
             lambda: meet(q, at, p, every),
@@ -276,9 +289,9 @@
         )
 
     def pair_share(p, q, second, ch):
-        at = pl.ds(ch * CROWS, CROWS)
-        upto = pl.ds(0, (ch + 1) * CROWS)
-        under = pl.ds(0, ch * CROWS)
+        at = span(ch)
+        upto = pl.ds(0, EDGES[ch + 1])
+        under = pl.ds(0, EDGES[ch])
 
         def roles(rows, cols):
             def first():
@@ -318,15 +331,11 @@
     for k in range(16):
         table[k:k + 1, :] = top[:, k * 128:(k + 1) * 128]
     values = split3(table[...])
-    for part in range(4):
-        index = jnp.concatenate([codes_of(part * 8 + k) for k in range(8)], axis=1) - 1
-        fine = jnp.where((index & 127) == lax.broadcasted_iota(I32, (128, 1024), 0), 1.0, 0.0).astype(BF)
-        found = jnp.dot(values, fine, preferred_element_type=F32)
-        found = (found[0:16] + found[16:32]) + found[32:48]
-        coarse = (index >> 7) == lax.broadcasted_iota(I32, (16, 1024), 0)
-        line = jnp.sum(jnp.where(coarse, found, 0.0), axis=0, keepdims=True)
-        for k in range(8):
-            answer[part * 8 + k] = line[:, k * 128:(k + 1) * 128]
+    found = jnp.dot(values, fine[...], preferred_element_type=F32)
+    found = (found[0:16] + found[16:32]) + found[32:48]
+    line = jnp.sum(jnp.where(coarse[...] > 0.5, found, 0.0), axis=0, keepdims=True)
+    for k in range(32):
+        answer[k] = line[:, k * 128:(k + 1) * 128]
 
     def send_answer(other, column):
         pltpu.make_async_remote_copy(
@@ -387,6 +396,8 @@
             pltpu.VMEM((4, 1, ROWS), F32),
             pltpu.VMEM((4, 1, ROWS), F32),
             pltpu.VMEM((16, 128), F32),
+            pltpu.VMEM((128, DEV * CAP), BF),
+            pltpu.VMEM((16, DEV * CAP), F32),
             pltpu.VMEM((32, 1, 128), F32),
             pltpu.VMEM((DEV, 1, 128), F32),
             pltpu.VMEM((128, DEV), F32),

time: 60.2 us -> 59.9 us (level)
  no operation moved by 1% of the time
where the time goes in v4:
time: 59.9 us; the launch traced here: 59.8 us
  Pallas kernels  58.5 us (98%)
  local copies, waits for them, and re-layouts  1.3 us (2%)
    pallas_call x1, Pallas kernels, shards(): pl.pallas_call(kernel, out_shape=jax.ShapeDtypeStruct((1, ROWS), F32), in...  58.5 us
    unnamed x1, local copies, waits for them, and re-layouts  1.3 us

profile of v4, /device:TPU:1, one launch (start us, length us, event | category | flops | bytes accessed | tf_op | source)
XLA Modules:
  0.0 59.8 jit_solution(4604481079720426368)
XLA Ops:
  0.0 58.5 %shard_map.55 = f32[1,2048]{1,0:T(1,128)} custom-call(bf16[2048,128]{1,0:T(8,128)(2,1)} %emb_hbm.1, s32[1,2048]{1,0:T(1,128)} %bitcast.4, s32[1,2048]{1,0:T(1,128)} %bitcast.5, s32[32]{0:T(128)} %size_hbm.1, s32[32]{0:T(128)} %owner_hbm.1), custom_call_target="tpu_custom_call" | custom-call | flops 12000000000 | bytes 1048576 | tf_op jit(solution)/shard_map/pallas_call | solution.py:370
  58.5 1.3 %copy.7 = f32[2048]{0:T(1024)} copy(f32[2048]{0:T(1024)} %bitcast.3) | data formatting | bytes 16384

commit v5 on v4

--- a/solution.py
+++ b/solution.py
@@ -66,9 +66,9 @@
 
     barrier = pltpu.get_barrier_semaphore()
 
-    def to_all(act):
+    def to_all(act, stride=1):
         def line(i, carry):
-            other = rem(dp + i, 16)
+            other = rem(dp + stride * i, 16)
             for j in range(8):
                 act(other, rem(nar + j, 8))
             return carry
@@ -343,7 +343,7 @@
             device_id=(other, column), device_id_type=MESH,
         ).start()
 
-    to_all(send_answer)
+    to_all(send_answer, 5)
     pltpu.make_async_copy(answer.at[div(me, 4)], answer_in.at[me], recv_ans).start()
     pltpu.make_async_copy(answer_in, answer_in, recv_ans).wait()
 

time: 59.9 us -> 59.6 us (level)
  no operation moved by 1% of the time
where the time goes in v5:
time: 59.6 us; the launch traced here: 59.5 us
  Pallas kernels  58.2 us (98%)
  local copies, waits for them, and re-layouts  1.3 us (2%)
    pallas_call x1, Pallas kernels, shards(): pl.pallas_call(kernel, out_shape=jax.ShapeDtypeStruct((1, ROWS), F32), in...  58.2 us
    unnamed x1, local copies, waits for them, and re-layouts  1.3 us

profile of v5, /device:TPU:1, one launch (start us, length us, event | category | flops | bytes accessed | tf_op | source)
XLA Modules:
  0.0 59.5 jit_solution(16168504826920334321)
XLA Ops:
  0.0 58.2 %shard_map.55 = f32[1,2048]{1,0:T(1,128)} custom-call(bf16[2048,128]{1,0:T(8,128)(2,1)} %emb_hbm.1, s32[1,2048]{1,0:T(1,128)} %bitcast.4, s32[1,2048]{1,0:T(1,128)} %bitcast.5, s32[32]{0:T(128)} %size_hbm.1, s32[32]{0:T(128)} %owner_hbm.1), custom_call_target="tpu_custom_call" | custom-call | flops 12000000000 | bytes 1048576 | tf_op jit(solution)/shard_map/pallas_call | solution.py:370
  58.2 1.3 %copy.7 = f32[2048]{0:T(1024)} copy(f32[2048]{0:T(1024)} %bitcast.3) | data formatting | bytes 16384
